TPU v7x, 32 devices: a whole 2x2x4 slice. The times are simulated.
32 devices in a mesh: col: 4 (over x, core), grp: 8 (over z, y).
Axes of the slice: x: 2, y: 2, z: 4, core: 2. Of those that a mesh axis runs over, the one named last changes fastest.
Arguments:
- grid_fields: bfloat16 [1024, 512], P(('col', 'grp')), may hold values from -6 to 6
- brick_slot: int32 [1024], P('col'), may hold values from 0 to 255, as said below
- block_brick: int32 [1024], P(('col', 'grp')), may hold values from 0 to 287, as said below
- node_mask: int32 [1024, 64], P(('col', 'grp')), may hold values 0 or 1
- counts: int32 [1024], P(('col', 'grp')), may hold values from 1 to 128, as said below
- shape_t: bfloat16 [1024, 64, 128], P(('col', 'grp')), may hold values from 0 to 0.099609375
- part_mass: float32 [1024, 128], P(('col', 'grp')), may hold values from 0.5 to 2
- part_vel: float32 [1024, 3, 128], P(('col', 'grp')), may hold values from -6 to 6
Outputs:
- vel_new: float32 [1024, 3, 128], P(('col', 'grp'))
- grid_momentum: float32 [1024, 256], P(('col', 'grp'))
Inputs may be any that keep to these rules, and one draw needn't show every extreme that they name: `brick_slot`: each aligned run of 256 entries is a permutation of 0 .. 255. `block_brick`: the first block of each device refers to a left neighbour brick, the second to a right neighbour brick, all others to bricks of the column itself; of one device's blocks at most 4 refer to bricks stored on any one device of the column, and exactly 4 to some device. `counts`: the first block of each device is full.
All inputs are finite; a program needn't handle non-finite values. No bound on the sum of `node_mask` on one device may be relied on, other than what follows from the above.
Results may differ from a plain program's by a relative error of at most 0.00041.
Values may be sent and summed in bfloat16 or wider, within the bound.
A program may use at most 64 MiB of HBM per device.

v0:
```python
import jax
import jax.numpy as jnp
from jax import lax
from jax.sharding import PartitionSpec as P

NODES = 64
FIELDS = 8
OUTF = 4
PBLK = 128
RIM = 16


def with_halo(cells, sides, width):
    for axis, dim in sides:
        count = lax.axis_size(axis)
        ends = count - 1
        head = lax.slice_in_dim(cells, 0, width, axis=dim)
        tail = lax.slice_in_dim(cells, cells.shape[dim] - width, cells.shape[dim], axis=dim)
        cells = jnp.concatenate(
            [
                lax.ppermute(tail, axis, [(i, (i + 1) % count) for i in range(ends)]),
                cells,
                lax.ppermute(head, axis, [((i + 1) % count, i) for i in range(ends)]),
            ],
            axis=dim,
        )
    return cells


def local(grid_fields, brick_slot, block_brick, node_mask, counts, shape_t, part_mass, part_vel):
    columns = brick_slot.shape[0]
    blocks = block_brick.shape[0]
    local_rows = grid_fields.shape[0]
    groups = lax.axis_size("grp")
    slots_each = max(2, (blocks - 2 + groups - 1) // groups)
    own_index = block_brick - RIM
    is_own = (own_index >= 0) & (own_index < columns)
    own_slot = jnp.take(brick_slot, jnp.clip(own_index, 0, columns - 1))
    owner = jnp.where(is_own, own_slot // local_rows, -1)
    row_at = own_slot % local_rows
    order = jnp.arange(blocks, dtype=jnp.int32)
    earlier = (owner[:, None] == owner[None, :]) & (order[None, :] < order[:, None])
    rank = jnp.sum(earlier.astype(jnp.int32), axis=1)
    dest = jnp.where(is_own, owner * slots_each + rank, groups * slots_each)
    edge_ids = jnp.concatenate(
        [jnp.arange(RIM, dtype=jnp.int32), jnp.arange(columns - RIM, columns, dtype=jnp.int32)]
    )
    edge_slot = jnp.take(brick_slot, edge_ids)
    mine = edge_slot // local_rows == lax.axis_index("grp")
    edge_match = mine[:, None] & (
        (edge_slot % local_rows)[:, None] == jnp.arange(local_rows, dtype=jnp.int32)[None, :]
    )
    gathered = lax.all_gather(grid_fields, "grp", axis=0, tiled=True)
    logical = jnp.take(gathered, brick_slot, axis=0)
    rims = jnp.concatenate([logical[:RIM], logical[columns - RIM :]], axis=0)
    wider = with_halo(rims, (("col", 0),), RIM)
    left_in = wider[:RIM]
    right_in = wider[3 * RIM :]
    extended = jnp.concatenate([left_in, logical, right_in], axis=0)
    block_rows = jnp.take(extended, block_brick, axis=0)
    weights = shape_t * node_mask[:, :, None].astype(jnp.bfloat16)
    block_fields = block_rows.reshape(blocks, FIELDS, NODES)
    interp = jnp.einsum("bfn,bnp->bfp", block_fields, weights, preferred_element_type=jnp.float32)
    live = (jnp.arange(PBLK, dtype=jnp.int32)[None, :] < counts[:, None]).astype(jnp.float32)
    blend = 0.4 * interp[:, 0:3] + 0.6 * (part_vel + interp[:, 3:6])
    vel_next = blend / (1.0 + 0.5 * interp[:, 7:8] * interp[:, 7:8]) * live[:, None, :]
    first = part_mass * (1.0 + 0.5 * jnp.tanh(interp[:, 6])) * live
    contrib = jnp.concatenate([first[:, None, :], part_mass[:, None, :] * vel_next], axis=1).astype(
        jnp.bfloat16
    )
    partial_value = jnp.einsum("bfp,bnp->bfn", contrib, weights, preferred_element_type=jnp.float32)
    partial_value = partial_value.reshape(blocks, OUTF * NODES)
    rim_index = jnp.where(block_brick < RIM, block_brick, block_brick - columns)
    rim_hit = (
        (jnp.arange(2 * RIM, dtype=jnp.int32)[:, None] == rim_index[None, :]) & (~is_own)[None, :]
    ).astype(jnp.float32)
    outgoing = jnp.dot(
        rim_hit, partial_value, precision=lax.Precision.HIGHEST, preferred_element_type=jnp.float32
    )
    incoming = with_halo(outgoing, (("col", 0),), RIM)
    edge_in = jnp.concatenate([incoming[:RIM], incoming[3 * RIM :]], axis=0)
    totals = lax.psum(edge_in, "grp")
    send_rows = (
        jnp.zeros((groups * slots_each, OUTF * NODES), jnp.float32)
        .at[dest]
        .set(partial_value, mode="drop")
    )
    send_index = jnp.full((groups * slots_each,), -1, jnp.int32).at[dest].set(row_at, mode="drop")
    got_rows, got_index = (
        lax.all_to_all(
            send_rows.reshape(groups, slots_each, OUTF * NODES),
            "grp",
            split_axis=0,
            concat_axis=0,
            tiled=True,
        ),
        lax.all_to_all(
            send_index.reshape(groups, slots_each), "grp", split_axis=0, concat_axis=0, tiled=True
        ),
    )
    place = (
        jnp.arange(local_rows, dtype=jnp.int32)[:, None] == got_index.reshape(-1)[None, :]
    ).astype(jnp.float32)
    momentum = jnp.dot(
        place,
        got_rows.reshape(groups * slots_each, OUTF * NODES),
        precision=lax.Precision.HIGHEST,
        preferred_element_type=jnp.float32,
    )
    momentum = momentum + jnp.dot(
        edge_match.astype(jnp.float32).T,
        totals,
        precision=lax.Precision.HIGHEST,
        preferred_element_type=jnp.float32,
    )
    return (vel_next, momentum)


def solution(mesh):
    placed = (
        P(("col", "grp"), None),
        P("col"),
        P(("col", "grp")),
        P(("col", "grp"), None),
        P(("col", "grp")),
        P(("col", "grp"), None, None),
        P(("col", "grp"), None),
        P(("col", "grp"), None, None),
    )
    return jax.shard_map(
        local,
        mesh=mesh,
        in_specs=placed,
        out_specs=(P(("col", "grp"), None, None), P(("col", "grp"), None)),
        check_vma=False,
    )
```

profile of v0, /device:TPU:2, one launch (start us, length us, event | category | flops | bytes accessed | tf_op | source)
XLA Modules:
  0.0 105.9 jit_solution(12257198432379632999)
XLA Ops:
  0.6 0.0 copy-start
  0.6 0.7 compare_select_fusion
  1.4 0.0 copy-done
  1.4 31.3 %all_gather.3 = bf16[256,512]{1,0:T(8,128)(2,1)S(1)} all-gather(bf16[32,512]{1,0:T(8,128)(2,1)} %param.10), channel_id=1, replica_groups=mesh['col'=4,'grp'=8] {'grp'}, dimensions={0}, use_global_device_ids=true | all-gather | bytes 294912 | tf_op jit(solution)/shard_map/all_gather | solution.py:53
  32.7 1.2 %gather_fusion = bf16[256,512]{1,0:T(8,128)(2,1)S(1)} fusion(bf16[256,512]{1,0:T(8,128)(2,1)S(1)} %all_gather.3, s32[1024]{0:T(1024)S(1)} %pad_clamp_fusion.3), kind=kCustom, calls=%fused_computation.2 | custom fusion | bytes 525312 | tf_op jit(solution)/shard_map/jit(_take)/gather | solution.py:54
  33.9 0.1 broadcast_select_fusion
  34.0 0.0 copy-start.4
  34.0 1.9 %collective-permute-start = (bf16[16,512]{1,0:T(8,128)(2,1)S(1)}, bf16[16,512]{1,0:T(8,128)(2,1)S(1)}, u32[]{:S(2)}, u32[]{:S(2)}) collective-permute-start(bf16[16,512]{1,0:T(8,128)(2,1)S(1)} %get-tuple-element.17), channel_id=1, source_target_pairs={{0,8},{8,16},{16,24},{1,9},{9,17},{17,25},{2,10},{10,18},{18,26},{... | collective-permute-start | bytes 49160 | tf_op jit(solution)/shard_map/ppermute | solution.py:21
  35.9 3.6 %collective-permute-start.1 = (bf16[16,512]{1,0:T(8,128)(2,1)S(1)}, bf16[16,512]{1,0:T(8,128)(2,1)S(1)}, u32[]{:S(2)}, u32[]{:S(2)}) collective-permute-start(bf16[16,512]{1,0:T(8,128)(2,1)S(1)} %get-tuple-element.18), channel_id=1, source_target_pairs={{8,0},{16,8},{24,16},{9,1},{17,9},{25,17},{10,2},{18,10},{26,18},{... | collective-permute-start | bytes 49160 | tf_op jit(solution)/shard_map/ppermute | solution.py:23
  39.6 0.0 copy-done.4
  39.6 0.7 gather_fusion.2
  40.4 0.2 convert_reduce_fusion
  40.5 0.7 scatter_custom_fusion
  41.2 0.7 all_to_all.9
  41.9 5.6 %all-to-all-start = ((s32[8,1,4]{2,1,0:T(1,128)}), s32[8,1,4]{2,1,0:T(1,128)S(1)}, u32[]{:S(2)}, u32[]{:S(2)}) async-start(s32[8,1,4]{2,1,0:T(1,128)} %bitcast.1), calls=%async_computation | async-start | bytes 8192 | tf_op jit(solution)/shard_map/all_to_all | solution.py:97
  47.5 0.0 copy-start.5
  47.5 0.6 copy-done.5
  48.2 0.1 fusion.21
  48.2 0.1 compare_select_fusion.1
  48.3 0.0 copy-start.3
  48.3 0.7 gather_fusion.3
  49.0 0.0 copy-start.6
  49.0 0.1 fusion.36
  49.1 0.0 copy-done.3
  49.2 0.0 collective-permute-done
  49.2 0.0 collective-permute-done.1
  49.2 0.6 gather_fusion.1
  49.8 0.1 gather.15
  50.0 0.1 copy-done.6
  50.1 0.7 fusion.2
  50.7 0.0 copy-start.1
  50.7 0.1 fusion.18
  50.8 0.0 copy-start.2
  50.8 0.6 copy-done.1
  51.5 0.1 fusion.29
  51.6 0.0 copy-done.2
  51.6 0.1 multiply_convert_fusion
  51.7 0.5 fusion
  52.2 0.1 reshape.120
  52.3 0.1 fusion.27
  52.4 1.9 %collective-permute-start.2 = (f32[16,256]{1,0:T(8,128)S(1)}, f32[16,256]{1,0:T(8,128)S(1)}, u32[]{:S(2)}, u32[]{:S(2)}) collective-permute-start(f32[16,256]{1,0:T(8,128)S(1)} %get-tuple-element.21), channel_id=1, source_target_pairs={{0,8},{8,16},{16,24},{1,9},{9,17},{17,25},{2,10},{10,18},{18,26},{... | collective-permute-start | bytes 49160 | tf_op jit(solution)/shard_map/ppermute | solution.py:21
  54.4 3.6 %collective-permute-start.3 = (f32[16,256]{1,0:T(8,128)S(1)}, f32[16,256]{1,0:T(8,128)S(1)}, u32[]{:S(2)}, u32[]{:S(2)}) collective-permute-start(f32[16,256]{1,0:T(8,128)S(1)} %get-tuple-element.22), channel_id=1, source_target_pairs={{8,0},{16,8},{24,16},{9,1},{17,9},{25,17},{10,2},{18,10},{26,18},{... | collective-permute-start | bytes 49160 | tf_op jit(solution)/shard_map/ppermute | solution.py:23
  58.0 0.0 all-to-all-done
  58.0 0.5 broadcast.117
  58.6 0.7 reduce.3
  59.2 0.1 eq.68
  59.3 0.7 scatter_custom_fusion.1
  60.0 0.6 reshape.74
  60.7 6.0 %all-to-all-start.1 = ((f32[8,4,256]{2,1,0:T(4,128)}), f32[8,4,256]{2,1,0:T(4,128)S(1)}, u32[]{:S(2)}, u32[]{:S(2)}) async-start(f32[8,4,256]{2,1,0:T(4,128)} %reshape.74), calls=%async_computation.1 | async-start | bytes 65536 | tf_op jit(solution)/shard_map/all_to_all | solution.py:90
  66.7 0.6 copy.23
  67.3 0.0 collective-permute-done.2
  67.3 0.0 collective-permute-done.3
  67.3 37.6 %psum.7 = f32[32,256]{1,0:T(8,128)S(1)} all-reduce(f32[32,256]{1,0:T(8,128)S(1)} %pad_maximum_fusion.1), channel_id=1, replica_groups=mesh['col'=4,'grp'=8] {'grp'}, use_global_device_ids=true, to_apply=%region_3.5 | all-reduce | flops 8192 | bytes 65536 | tf_op jit(solution)/shard_map/psum | solution.py:82
  104.9 0.0 all-to-all-done.1
  104.9 0.1 fusion.22
  105.0 0.9 convolution_add_fusion
  (20 shorter events, 0.2 us)
Async XLA Ops:
  0.6 0.8 copy-start
  34.0 5.6 %copy-start.4 = (s32[32]{0:T(128)S(1)}, s32[32]{0:T(128)}, u32[]{:S(2)}) copy-start(s32[32]{0:T(128)} %param.12) | copy-start | bytes 388
  34.0 15.2 %collective-permute-start = (bf16[16,512]{1,0:T(8,128)(2,1)S(1)}, bf16[16,512]{1,0:T(8,128)(2,1)S(1)}, u32[]{:S(2)}, u32[]{:S(2)}) collective-permute-start(bf16[16,512]{1,0:T(8,128)(2,1)S(1)} %get-tuple-element.17), channel_id=1, source_target_pairs={{0,8},{8,16},{16,24},{1,9},{9,17},{17,25},{2,10},{10,18},{18,26},{... | collective-permute-start | bytes 49160 | tf_op jit(solution)/shard_map/ppermute | solution.py:21
  35.9 13.3 %collective-permute-start.1 = (bf16[16,512]{1,0:T(8,128)(2,1)S(1)}, bf16[16,512]{1,0:T(8,128)(2,1)S(1)}, u32[]{:S(2)}, u32[]{:S(2)}) collective-permute-start(bf16[16,512]{1,0:T(8,128)(2,1)S(1)} %get-tuple-element.18), channel_id=1, source_target_pairs={{8,0},{16,8},{24,16},{9,1},{17,9},{25,17},{10,2},{18,10},{26,18},{... | collective-permute-start | bytes 49160 | tf_op jit(solution)/shard_map/ppermute | solution.py:23
  41.9 16.1 %all-to-all-start = ((s32[8,1,4]{2,1,0:T(1,128)}), s32[8,1,4]{2,1,0:T(1,128)S(1)}, u32[]{:S(2)}, u32[]{:S(2)}) async-start(s32[8,1,4]{2,1,0:T(1,128)} %bitcast.1), calls=%async_computation | async-start | bytes 8192 | tf_op jit(solution)/shard_map/all_to_all | solution.py:97
  47.5 0.7 copy-start.5
  48.3 0.8 copy-start.3
  49.0 1.0 copy-start.6
  50.7 0.7 copy-start.1
  50.8 0.8 copy-start.2
  52.4 14.8 %collective-permute-start.2 = (f32[16,256]{1,0:T(8,128)S(1)}, f32[16,256]{1,0:T(8,128)S(1)}, u32[]{:S(2)}, u32[]{:S(2)}) collective-permute-start(f32[16,256]{1,0:T(8,128)S(1)} %get-tuple-element.21), channel_id=1, source_target_pairs={{0,8},{8,16},{16,24},{1,9},{9,17},{17,25},{2,10},{10,18},{18,26},{... | collective-permute-start | bytes 49160 | tf_op jit(solution)/shard_map/ppermute | solution.py:21
  54.4 12.9 %collective-permute-start.3 = (f32[16,256]{1,0:T(8,128)S(1)}, f32[16,256]{1,0:T(8,128)S(1)}, u32[]{:S(2)}, u32[]{:S(2)}) collective-permute-start(f32[16,256]{1,0:T(8,128)S(1)} %get-tuple-element.22), channel_id=1, source_target_pairs={{8,0},{16,8},{24,16},{9,1},{17,9},{25,17},{10,2},{18,10},{26,18},{... | collective-permute-start | bytes 49160 | tf_op jit(solution)/shard_map/ppermute | solution.py:23
  60.7 44.2 %all-to-all-start.1 = ((f32[8,4,256]{2,1,0:T(4,128)}), f32[8,4,256]{2,1,0:T(4,128)S(1)}, u32[]{:S(2)}, u32[]{:S(2)}) async-start(f32[8,4,256]{2,1,0:T(4,128)} %reshape.74), calls=%async_computation.1 | async-start | bytes 65536 | tf_op jit(solution)/shard_map/all_to_all | solution.py:90
where the time goes:
time: 106 us
  blocking collectives  68.9 us (65%)
  starting transfers between devices  22.7 us (21%)
  local copies, waits for them, and re-layouts  8.86 us (8%)
  matrix products  2.29 us (2%)
  other arithmetic  2.28 us (2%)
    psum x1, blocking collectives, local(): totals = lax.psum(edge_in, 'grp')  37.6 us
    all_gather x1, blocking collectives, local(): gathered = lax.all_gather(grid_fields, 'grp', axis=0, tiled=True)  31.3 us
    ppermute x2, starting transfers between devices, with_halo(): lax.ppermute(head, axis, [((i + 1) % count, i) for i in range(ends)])  7.28 us
    all_to_all x1, starting transfers between devices, local(): lax.all_to_all(send_rows.reshape(groups, slots_each, OUTF * NODES), 'grp'...  6 us
    all_to_all x1, starting transfers between devices, local(): lax.all_to_all(send_index.reshape(groups, slots_each), 'grp', split_axis=...  5.58 us
    ppermute x2, starting transfers between devices, with_halo(): lax.ppermute(tail, axis, [(i, (i + 1) % count) for i in range(ends)])  3.84 us
  transfers between devices with their start and end apart: 6, of which 0 were waited for; matrix products, arithmetic and copies ran while one was open for 8% of the time, Pallas kernels for 0%

commit v1 on v0

--- a/solution.py
+++ b/solution.py
@@ -8,6 +8,11 @@
 OUTF = 4
 PBLK = 128
 RIM = 16
+
+
+def summed_here(x, axis):
+    parts = lax.all_gather(x, axis)
+    return jnp.sum(parts, axis=0)
 
 
 def with_halo(cells, sides, width):
@@ -79,7 +84,7 @@
     )
     incoming = with_halo(outgoing, (("col", 0),), RIM)
     edge_in = jnp.concatenate([incoming[:RIM], incoming[3 * RIM :]], axis=0)
-    totals = lax.psum(edge_in, "grp")
+    totals = summed_here(edge_in, "grp")
     send_rows = (
         jnp.zeros((groups * slots_each, OUTF * NODES), jnp.float32)
         .at[dest]

time: 106 us -> 100 us (0.943)
  blocking collectives: 68.9 us -> 62.7 us
    psum x1 -> x0, blocking collectives: 37.6 us -> none  [local(): totals = lax.psum(edge_in, 'grp')]
    all_gather x0 -> x1, blocking collectives: none -> 31.4 us  [summed_here(): parts = lax.all_gather(x, axis)]
where the time goes in v1:
time: 100 us; the launch traced here: 99.8 us
  blocking collectives  62.7 us (63%)
  starting transfers between devices  22.7 us (23%)
  local copies, waits for them, and re-layouts  8.86 us (9%)
  other arithmetic  2.3 us (2%)
  matrix products  2.29 us (2%)
    all_gather x1, blocking collectives, summed_here(): parts = lax.all_gather(x, axis)  31.4 us
    all_gather x1, blocking collectives, local(): gathered = lax.all_gather(grid_fields, 'grp', axis=0, tiled=True)  31.3 us
    ppermute x2, starting transfers between devices, with_halo(): lax.ppermute(head, axis, [((i + 1) % count, i) for i in range(ends)])  7.28 us
    all_to_all x1, starting transfers between devices, local(): lax.all_to_all(send_rows.reshape(groups, slots_each, OUTF * NODES), 'grp'...  6 us
    all_to_all x1, starting transfers between devices, local(): lax.all_to_all(send_index.reshape(groups, slots_each), 'grp', split_axis=...  5.58 us
    ppermute x2, starting transfers between devices, with_halo(): lax.ppermute(tail, axis, [(i, (i + 1) % count) for i in range(ends)])  3.84 us
    unnamed x15, local copies, waits for them, and re-layouts  2.12 us
  transfers between devices with their start and end apart: 6, of which 0 were waited for; matrix products, arithmetic and copies ran while one was open for 8% of the time, Pallas kernels for 0%

profile of v1, /device:TPU:2, one launch (start us, length us, event | category | flops | bytes accessed | tf_op | source)
XLA Modules:
  0.0 99.8 jit_solution(4209534792258660130)
XLA Ops:
  0.6 0.0 copy-start
  0.6 0.7 compare_select_fusion
  1.4 0.0 copy-done
  1.4 31.3 %all_gather.9 = bf16[256,512]{1,0:T(8,128)(2,1)S(1)} all-gather(bf16[32,512]{1,0:T(8,128)(2,1)} %param.10), channel_id=1, replica_groups=mesh['col'=4,'grp'=8] {'grp'}, dimensions={0}, use_global_device_ids=true | all-gather | bytes 294912 | tf_op jit(solution)/shard_map/all_gather | solution.py:58
  32.7 1.2 %gather_fusion = bf16[256,512]{1,0:T(8,128)(2,1)S(1)} fusion(bf16[256,512]{1,0:T(8,128)(2,1)S(1)} %all_gather.9, s32[1024]{0:T(1024)S(1)} %pad_clamp_fusion.3), kind=kCustom, calls=%fused_computation.2 | custom fusion | bytes 525312 | tf_op jit(solution)/shard_map/jit(_take)/gather | solution.py:59
  33.9 0.1 broadcast_select_fusion
  34.0 0.0 copy-start.4
  34.0 1.9 %collective-permute-start = (bf16[16,512]{1,0:T(8,128)(2,1)S(1)}, bf16[16,512]{1,0:T(8,128)(2,1)S(1)}, u32[]{:S(2)}, u32[]{:S(2)}) collective-permute-start(bf16[16,512]{1,0:T(8,128)(2,1)S(1)} %get-tuple-element.17), channel_id=1, source_target_pairs={{0,8},{8,16},{16,24},{1,9},{9,17},{17,25},{2,10},{10,18},{18,26},{... | collective-permute-start | bytes 49160 | tf_op jit(solution)/shard_map/ppermute | solution.py:26
  35.9 3.6 %collective-permute-start.1 = (bf16[16,512]{1,0:T(8,128)(2,1)S(1)}, bf16[16,512]{1,0:T(8,128)(2,1)S(1)}, u32[]{:S(2)}, u32[]{:S(2)}) collective-permute-start(bf16[16,512]{1,0:T(8,128)(2,1)S(1)} %get-tuple-element.18), channel_id=1, source_target_pairs={{8,0},{16,8},{24,16},{9,1},{17,9},{25,17},{10,2},{18,10},{26,18},{... | collective-permute-start | bytes 49160 | tf_op jit(solution)/shard_map/ppermute | solution.py:28
  39.6 0.0 copy-done.4
  39.6 0.7 gather_fusion.2
  40.4 0.2 convert_reduce_fusion
  40.5 0.7 scatter_custom_fusion
  41.2 0.7 all_to_all.9
  41.9 5.6 %all-to-all-start = ((s32[8,1,4]{2,1,0:T(1,128)}), s32[8,1,4]{2,1,0:T(1,128)S(1)}, u32[]{:S(2)}, u32[]{:S(2)}) async-start(s32[8,1,4]{2,1,0:T(1,128)} %bitcast.1), calls=%async_computation | async-start | bytes 8192 | tf_op jit(solution)/shard_map/all_to_all | solution.py:102
  47.5 0.0 copy-start.5
  47.5 0.6 copy-done.5
  48.2 0.1 fusion.21
  48.2 0.1 compare_select_fusion.1
  48.3 0.0 copy-start.3
  48.3 0.7 gather_fusion.3
  49.0 0.0 copy-start.6
  49.0 0.1 fusion.36
  49.1 0.0 copy-done.3
  49.2 0.0 collective-permute-done
  49.2 0.0 collective-permute-done.1
  49.2 0.6 gather_fusion.1
  49.8 0.1 gather.15
  50.0 0.1 copy-done.6
  50.1 0.7 fusion.2
  50.7 0.0 copy-start.1
  50.7 0.1 fusion.18
  50.8 0.0 copy-start.2
  50.8 0.6 copy-done.1
  51.5 0.1 fusion.29
  51.6 0.0 copy-done.2
  51.6 0.1 multiply_convert_fusion
  51.7 0.5 fusion
  52.2 0.1 reshape.120
  52.3 0.1 fusion.27
  52.4 1.9 %collective-permute-start.2 = (f32[16,256]{1,0:T(8,128)S(1)}, f32[16,256]{1,0:T(8,128)S(1)}, u32[]{:S(2)}, u32[]{:S(2)}) collective-permute-start(f32[16,256]{1,0:T(8,128)S(1)} %get-tuple-element.21), channel_id=1, source_target_pairs={{0,8},{8,16},{16,24},{1,9},{9,17},{17,25},{2,10},{10,18},{18,26},{... | collective-permute-start | bytes 49160 | tf_op jit(solution)/shard_map/ppermute | solution.py:26
  54.4 3.6 %collective-permute-start.3 = (f32[16,256]{1,0:T(8,128)S(1)}, f32[16,256]{1,0:T(8,128)S(1)}, u32[]{:S(2)}, u32[]{:S(2)}) collective-permute-start(f32[16,256]{1,0:T(8,128)S(1)} %get-tuple-element.22), channel_id=1, source_target_pairs={{8,0},{16,8},{24,16},{9,1},{17,9},{25,17},{10,2},{18,10},{26,18},{... | collective-permute-start | bytes 49160 | tf_op jit(solution)/shard_map/ppermute | solution.py:28
  58.0 0.0 all-to-all-done
  58.0 0.5 broadcast.117
  58.6 0.7 reduce.3
  59.2 0.1 eq.68
  59.3 0.7 scatter_custom_fusion.1
  60.0 0.6 reshape.74
  60.7 6.0 %all-to-all-start.1 = ((f32[8,4,256]{2,1,0:T(4,128)}), f32[8,4,256]{2,1,0:T(4,128)S(1)}, u32[]{:S(2)}, u32[]{:S(2)}) async-start(f32[8,4,256]{2,1,0:T(4,128)} %reshape.74), calls=%async_computation.1 | async-start | bytes 65536 | tf_op jit(solution)/shard_map/all_to_all | solution.py:95
  66.7 0.6 copy.23
  67.3 0.0 collective-permute-done.2
  67.3 0.0 collective-permute-done.3
  67.3 31.4 %all-gather = f32[256,256]{1,0:T(8,128)S(1)} all-gather(f32[32,256]{1,0:T(8,128)S(1)} %pad_maximum_fusion.1), channel_id=2, replica_groups=mesh['col'=4,'grp'=8] {'grp'}, dimensions={0}, use_global_device_ids=true | all-gather | bytes 294912 | tf_op jit(solution)/shard_map/all_gather | solution.py:14
  98.7 0.0 all-to-all-done.1
  98.7 0.1 fusion.22
  98.9 0.9 convolution_add_fusion
  (21 shorter events, 0.2 us)
Async XLA Ops:
  0.6 0.8 copy-start
  34.0 5.6 %copy-start.4 = (s32[32]{0:T(128)S(1)}, s32[32]{0:T(128)}, u32[]{:S(2)}) copy-start(s32[32]{0:T(128)} %param.12) | copy-start | bytes 388
  34.0 15.2 %collective-permute-start = (bf16[16,512]{1,0:T(8,128)(2,1)S(1)}, bf16[16,512]{1,0:T(8,128)(2,1)S(1)}, u32[]{:S(2)}, u32[]{:S(2)}) collective-permute-start(bf16[16,512]{1,0:T(8,128)(2,1)S(1)} %get-tuple-element.17), channel_id=1, source_target_pairs={{0,8},{8,16},{16,24},{1,9},{9,17},{17,25},{2,10},{10,18},{18,26},{... | collective-permute-start | bytes 49160 | tf_op jit(solution)/shard_map/ppermute | solution.py:26
  35.9 13.3 %collective-permute-start.1 = (bf16[16,512]{1,0:T(8,128)(2,1)S(1)}, bf16[16,512]{1,0:T(8,128)(2,1)S(1)}, u32[]{:S(2)}, u32[]{:S(2)}) collective-permute-start(bf16[16,512]{1,0:T(8,128)(2,1)S(1)} %get-tuple-element.18), channel_id=1, source_target_pairs={{8,0},{16,8},{24,16},{9,1},{17,9},{25,17},{10,2},{18,10},{26,18},{... | collective-permute-start | bytes 49160 | tf_op jit(solution)/shard_map/ppermute | solution.py:28
  41.9 16.1 %all-to-all-start = ((s32[8,1,4]{2,1,0:T(1,128)}), s32[8,1,4]{2,1,0:T(1,128)S(1)}, u32[]{:S(2)}, u32[]{:S(2)}) async-start(s32[8,1,4]{2,1,0:T(1,128)} %bitcast.1), calls=%async_computation | async-start | bytes 8192 | tf_op jit(solution)/shard_map/all_to_all | solution.py:102
  47.5 0.7 copy-start.5
  48.3 0.8 copy-start.3
  49.0 1.0 %copy-start.6 = (bf16[32,64,128]{2,1,0:T(8,128)(2,1)S(1)}, bf16[32,64,128]{2,1,0:T(8,128)(2,1)}, u32[]{:S(2)}) copy-start(bf16[32,64,128]{2,1,0:T(8,128)(2,1)} %param.15) | copy-start | bytes 1572868
  50.7 0.7 copy-start.1
  50.8 0.8 copy-start.2
  52.4 14.8 %collective-permute-start.2 = (f32[16,256]{1,0:T(8,128)S(1)}, f32[16,256]{1,0:T(8,128)S(1)}, u32[]{:S(2)}, u32[]{:S(2)}) collective-permute-start(f32[16,256]{1,0:T(8,128)S(1)} %get-tuple-element.21), channel_id=1, source_target_pairs={{0,8},{8,16},{16,24},{1,9},{9,17},{17,25},{2,10},{10,18},{18,26},{... | collective-permute-start | bytes 49160 | tf_op jit(solution)/shard_map/ppermute | solution.py:26
  54.4 12.9 %collective-permute-start.3 = (f32[16,256]{1,0:T(8,128)S(1)}, f32[16,256]{1,0:T(8,128)S(1)}, u32[]{:S(2)}, u32[]{:S(2)}) collective-permute-start(f32[16,256]{1,0:T(8,128)S(1)} %get-tuple-element.22), channel_id=1, source_target_pairs={{8,0},{16,8},{24,16},{9,1},{17,9},{25,17},{10,2},{18,10},{26,18},{... | collective-permute-start | bytes 49160 | tf_op jit(solution)/shard_map/ppermute | solution.py:28
  60.7 38.0 %all-to-all-start.1 = ((f32[8,4,256]{2,1,0:T(4,128)}), f32[8,4,256]{2,1,0:T(4,128)S(1)}, u32[]{:S(2)}, u32[]{:S(2)}) async-start(f32[8,4,256]{2,1,0:T(4,128)} %reshape.74), calls=%async_computation.1 | async-start | bytes 65536 | tf_op jit(solution)/shard_map/all_to_all | solution.py:95
